TPU v7x, 32 devices: a whole 2x2x4 slice. The times are simulated.
32 devices in a mesh: gx: 4 (over y, core), gy: 4 (over z), gz: 2 (over x).
Axes of the slice: x: 2, y: 2, z: 4, core: 2. Of those that a mesh axis runs over, the one named last changes fastest.
Arguments:
- scalars: float32 [4, 4, 2, 128, 128], P('gx', 'gy', 'gz'), may hold values from -6 to 6
- vectors: float32 [4, 4, 2, 3, 128, 128], P('gx', 'gy', 'gz'), may hold values from -6 to 6
- positions: float32 [4, 4, 2, 3, 128], P('gx', 'gy', 'gz'), may hold values from 0 to 6
- species: int32 [4, 4, 2, 128], P('gx', 'gy', 'gz'), may hold values from 0 to 7
- atom_count: int32 [4, 4, 2], P('gx', 'gy', 'gz'), may hold values from 64 to 128, as said below
- energy_weight: float32 [4, 4, 2, 128], P('gx', 'gy', 'gz'), may hold values from -5 to 5
- local_pairs: int32 [4, 4, 2, 2, 1024], P('gx', 'gy', 'gz'), may hold values from 0 to 127, as said below
- face_pairs: int32 [4, 4, 2, 3, 2, 256], P('gx', 'gy', 'gz'), may hold values from 0 to 127, as said below
- tile_counts: int32 [4, 4, 2, 4], P('gx', 'gy', 'gz'), may hold values from 85 to 1024, as said below
- w_center: float32 [128, 128], replicated, may hold values from -0.5 to 0.5
- w_partner: float32 [128, 128], replicated, may hold values from -0.5 to 0.5
- w_radial: float32 [8, 128], replicated, may hold values from -4 to 4
- species_embed: float32 [2, 8, 128], replicated, may hold values from -3 to 3
- w_mix: float32 [128, 128], replicated, may hold values from -0.5 to 0.5
- w_channel: float32 [2, 128, 128], replicated, may hold values from -0.5 to 0.5
- w_read: float32 [128, 128], replicated, may hold values from -0.5 to 0.5
- w_out: float32 [128], replicated, may hold values from -0.5 to 0.5
- species_energy: float32 [8], replicated, may hold values from -2 to 2
Outputs:
- atom_energy: float32 [4, 4, 2, 128], P('gx', 'gy', 'gz')
- position_grad: float32 [4, 4, 2, 3, 128], P('gx', 'gy', 'gz')
- scalar_grad: float32 [4, 4, 2, 128, 128], P('gx', 'gy', 'gz')
- vector_grad: float32 [4, 4, 2, 3, 128, 128], P('gx', 'gy', 'gz')
- weight_grad: float32 [101512], replicated
Inputs may be any that keep to these rules, and one draw needn't show every extreme that they name: `atom_count`: some domain holds exactly 128 live atoms; slots at or above a domain's count are padding. `tile_counts`: entry 0 counts the live slots of the local tile (at least 512), entries 1 to 3 those of the face tiles (at least 85); some domain fills all four tiles. `local_pairs`: every slot names two different atoms of the domain, both below its atom count; live slots are those below tile_counts[0]. `face_pairs`: in tile d, entry 0 names an atom below this domain's count and entry 1 an atom below the count of the next domain along grid direction d (wrapping around); live slots are those below tile_counts[1 + d].
All inputs are finite; a program needn't handle non-finite values.
Results may differ from a plain program's by a relative error of at most 0.0003.
Values sent between devices are 32-bit elements; how exact they have to be, the bound alone decides.
A program may use at most 128 MiB of HBM per device.

v0:
```python
import functools

import jax
import jax.numpy as jnp
from jax import lax
from jax.experimental import pallas as pl
from jax.experimental.pallas import tpu as pltpu
from jax.sharding import PartitionSpec as P

CUTOFF = 5.0
EDGE = 6.0
HIGHEST = lax.Precision.HIGHEST
F32 = jnp.float32
B16 = jnp.bfloat16
AXES = ("gx", "gy", "gz")
MESH = pl.DeviceIdType.MESH
ORDER = (1, 2, 0)


def split(x):
    hi = x.astype(B16)
    return hi, (x - hi.astype(F32)).astype(B16)


def weight3(w):
    hi, lo = split(w)
    return jnp.concatenate([hi, hi, lo], axis=1)


def stack3(pair):
    return jnp.concatenate([pair[0], pair[1], pair[0]], axis=0)


def mul(a, b):
    return jnp.dot(a, b, preferred_element_type=F32)


def mul_t(a, b, precision=None):
    return lax.dot_general(
        a, b, (((1,), (1,)), ((), ())), precision=precision, preferred_element_type=F32
    )


def outer3(x, g):
    left = jnp.concatenate([x[0], x[1], x[0]], axis=1)
    right = jnp.concatenate([g[0], g[0], g[1]], axis=1)
    return mul_t(left, right)


def gate(x):
    return 0.5 * jnp.tanh(0.5 * x) + 0.5


def rows_of(parts, count, width):
    row = lax.broadcasted_iota(jnp.int32, (count, width), 0)
    total = jnp.zeros((count, width), F32)
    for k, part in enumerate(parts):
        total = jnp.where(row == k, part, total)
    return total


def phase_list(sizes):
    nx, ny, nz = sizes
    phases = []
    if nx % 2 == 0 and nx > 2:
        phases += [("gx", 1, 2), ("gx", 2, nx // 2)]
    else:
        phases += [("gx", 1, nx)]
    phases += [("gz", 1, nz), ("gy", 1, ny)]
    return [p for p in phases if p[2] > 1]


def kernel(sizes, rows, block_pairs, *refs):
    phases = phase_list(sizes)
    n_phases = len(phases)
    (sc, vec, small, lp, fp, counts, atoms, wc, wp, wr, emb, wmix, wch, wread, wout, ref_e,
     energy_out, pos_out, sgrad_out, vgrad_out, wgrad_out,
     here, there, near, ret, back, acc_c, acc_p, gbuf, agb,
     mix_f, mix_b, ch_f, ch_b, read_f, read_b) = refs[:36]
    landing = refs[36:36 + n_phases]
    in_send, in_recv, ret_send, ret_recv, rs_send, rs_recv, ag_send, ag_recv = refs[36 + n_phases:]
    atom_slots = sc.shape[1]
    channels = sc.shape[0]
    species_count = wr.shape[0]
    index = {a: lax.axis_index(a) for a in AXES}

    def neighbour(d, step):
        n = sizes[d]
        return {AXES[d]: lax.rem(index[AXES[d]] + step + n, n)}

    def peer(phase, k):
        axis, stride, size = phase
        q = lax.rem(index[axis] // stride, size)
        t = lax.rem(q + k, size)
        return q, t, {axis: index[axis] + (t - q) * stride}

    greeted = []
    for d in range(3):
        greeted.append(neighbour(d, 1))
        if sizes[d] > 2:
            greeted.append(neighbour(d, -1))
    for phase in phases:
        for k in range(1, phase[2]):
            greeted.append(peer(phase, k)[2])
    barrier = pltpu.get_barrier_semaphore()
    for target in greeted:
        pl.semaphore_signal(barrier, inc=1, device_id=target, device_id_type=MESH)
    pl.semaphore_wait(barrier, len(greeted))

    inbound = {}
    for d in ORDER:
        copies = []
        for part, (src, lo, hi) in enumerate(((small, 512, 520), (sc, 0, 128), (vec, 128, 512))):
            copy = pltpu.make_async_remote_copy(
                src_ref=src,
                dst_ref=near.at[d, lo:hi],
                send_sem=in_send.at[3 * d + part],
                recv_sem=in_recv.at[3 * d + part],
                device_id=neighbour(d, -1),
                device_id_type=MESH,
            )
            copy.start()
            copies.append(copy)
        inbound[d] = copies

    mix_b[...] = weight3(wmix[...])
    mix_f[...] = weight3(wmix[...].T)
    read_b[...] = weight3(wread[...])
    read_f[...] = weight3(wread[...].T)
    ch_b[...] = weight3(jnp.concatenate([wch[0:128], wch[128:256]], axis=1))
    ch_f[...] = weight3(jnp.concatenate([wch[0:128].T, wch[128:256].T], axis=0))
    radial = wr[...]
    radial_t = jnp.concatenate([radial] * (channels // species_count), axis=0).T[:, 0:species_count]
    out_col = jnp.broadcast_to(wout[...], (channels, channels)).T[:, 0:1]
    wc_t = weight3(wc[...].T)
    wp_t = weight3(wp[...].T)
    gbuf[...] = jnp.zeros_like(gbuf)
    acc_c[...] = jnp.zeros_like(acc_c)
    acc_p[...] = jnp.zeros_like(acc_p)

    def hot_of(small_rows):
        row = lax.broadcasted_iota(jnp.int32, (species_count, atom_slots), 0).astype(F32)
        return (row == small_rows[4:5]).astype(F32)

    def embed(table, hot):
        return lax.dot_general(
            table, hot, (((0,), (0,)), ((), ())), precision=HIGHEST, preferred_element_type=F32
        )

    def fill(dst, proj, vectors, small_rows):
        hi, lo = split(proj)
        dst[0:128, 0:128] = hi
        dst[0:128, 128:256] = lo
        hi, lo = split(vectors)
        dst[128:512, 0:128] = hi
        dst[128:512, 128:256] = lo
        hi, lo = split(small_rows)
        hi, lo = hi.astype(F32), lo.astype(F32)
        rest = small_rows - hi - lo
        top = jnp.concatenate([hi, lo], axis=1)
        low = jnp.concatenate([rest, jnp.zeros_like(rest)], axis=1)
        dst[512:528, :] = jnp.concatenate([top, low], axis=0).astype(B16)

    hot = hot_of(small)
    sc3 = stack3(split(sc[...]))
    fill(here, mul(wc_t, sc3) + embed(emb[0:8], hot), vec[...], small[...])
    fill(there, mul(wp_t, sc3) + embed(emb[8:16], hot), vec[...], small[...])

    width = block_pairs
    spacing = CUTOFF * CUTOFF / (species_count - 1)

    def block(ii, jj, live, offsets):
        lane_atoms = lax.broadcasted_iota(jnp.int32, (atom_slots, width), 0)
        oi = (lane_atoms == ii).astype(F32).astype(B16)
        oj = (lane_atoms == jj).astype(F32).astype(B16)
        at_i = mul(here[...], jnp.concatenate([oi, oi], axis=0))
        at_j = mul(there[...], jnp.concatenate([oj, oj], axis=0))
        si = at_i[512:520] + at_i[520:528]
        sj = at_j[512:520] + at_j[520:528]
        cv = [at_i[128 * (k + 1):128 * (k + 2)] for k in range(3)]
        pv = [at_j[128 * (k + 1):128 * (k + 2)] for k in range(3)]
        d = [sj[k:k + 1] + offsets[k] - si[k:k + 1] for k in range(3)]
        pair_weight = si[3:4] + sj[3:4]
        sq = d[0] * d[0] + d[1] * d[1] + d[2] * d[2]
        order = lax.broadcasted_iota(jnp.int32, (species_count, width), 0).astype(F32)
        t = (sq - order * spacing) / spacing
        basis = jnp.exp(-(t * t))
        latent = at_i[0:128] + at_j[0:128] + jnp.dot(
            radial_t, basis, precision=HIGHEST, preferred_element_type=F32
        )
        s1 = gate(latent)
        first = latent * s1
        first2 = split(first)
        m = mul(mix_f[...], stack3(first2))
        s2 = gate(m)
        second = first + m * s2
        second2 = split(second)
        gains = mul(ch_f[...], stack3(second2))
        vg, tg = gains[0:128], gains[128:256]
        n = [x * (1.0 / CUTOFF) for x in d]
        ap = n[0] * pv[0] + n[1] * pv[1] + n[2] * pv[2]
        ac = n[0] * cv[0] + n[1] * cv[1] + n[2] * cv[2]
        ip = cv[0] * pv[0] + cv[1] * pv[1] + cv[2] * pv[2]
        ss = sq * (1.0 / (CUTOFF * CUTOFF))
        third = ss * (1.0 / 3.0)
        q = ac * ap - third * ip
        mixed = second + vg * ap + tg * q
        mixed2 = split(mixed)
        u = mul(read_f[...], stack3(mixed2))
        s3 = gate(u)
        h = u * s3
        readout = jnp.sum(out_col * h, axis=0, keepdims=True)
        env = 1.0 / (1.0 + ss)
        half_live = 0.5 * live
        halves = half_live * env * readout
        ge = half_live * pair_weight
        gr = ge * env
        gbuf[792:800] += mul_t(rows_of([gr], 8, width), h, HIGHEST)
        du = (out_col * gr) * (s3 * (1.0 + u * (1.0 - s3)))
        du2 = split(du)
        gbuf[664:792] += outer3(mixed2, du2)
        dmixed = mul(read_b[...], stack3(du2))
        dq = dmixed * tg
        dap = dmixed * vg + dq * ac
        dac = dq * ap
        dip = -third * dq
        dss = -jnp.sum(dq * ip, axis=0, keepdims=True) * (1.0 / 3.0)
        dgain2 = split(jnp.concatenate([dmixed * ap, dmixed * q], axis=0))
        dch = outer3(second2, dgain2)
        gbuf[408:536] += dch[:, 0:128]
        gbuf[536:664] += dch[:, 128:256]
        dsecond = dmixed + mul(ch_b[...], stack3(dgain2))
        dm = dsecond * (s2 * (1.0 + m * (1.0 - s2)))
        dm2 = split(dm)
        gbuf[280:408] += outer3(first2, dm2)
        dfirst = dsecond + mul(mix_b[...], stack3(dm2))
        dlat = dfirst * (s1 * (1.0 + latent * (1.0 - s1)))
        gbuf[256:264] += mul_t(basis, dlat, HIGHEST)
        dbasis = jnp.dot(radial, dlat, precision=HIGHEST, preferred_element_type=F32)
        dsq = jnp.sum(dbasis * basis * t, axis=0, keepdims=True) * (-2.0 / spacing)
        dsq = dsq + (dss - ge * readout * env * env) * (1.0 / (CUTOFF * CUTOFF))
        dcv = [n[k] * dac + dip * pv[k] for k in range(3)]
        dpv = [n[k] * dap + dip * cv[k] for k in range(3)]
        dd = [
            jnp.sum(dac * cv[k] + dap * pv[k], axis=0, keepdims=True) * (1.0 / CUTOFF)
            + 2.0 * d[k] * dsq
            for k in range(3)
        ]
        lat2 = split(dlat)

        def scatter(vector_parts, small_parts, one_hot):
            pieces = [lat2] + [split(v) for v in vector_parts]
            pieces.append(split(rows_of(small_parts, 16, width)))
            his = jnp.concatenate([p[0] for p in pieces], axis=0)
            los = jnp.concatenate([p[1] for p in pieces], axis=0)
            return mul_t(
                jnp.concatenate([his, los], axis=1), jnp.concatenate([one_hot, one_hot], axis=1)
            )

        acc_c[...] += scatter(dcv, [-dd[0], -dd[1], -dd[2], halves], oi)
        return scatter(dpv, dd + [halves], oj)

    slot = lax.broadcasted_iota(jnp.int32, (1, width), 1)

    def local_step(step, carry):
        start = pl.multiple_of(step * width, width)
        pairs = lp[:, pl.ds(start, width)]
        live = (slot + start < counts[0]).astype(F32)
        acc_p[...] += block(pairs[0:1], pairs[1:2], live, (0.0, 0.0, 0.0))
        return carry

    lax.fori_loop(0, lp.shape[1] // width, local_step, 0)

    sc2 = split(sc[...])
    gbuf[128:256] += outer3(sc2, split(acc_p[0:128]))
    gbuf[272:280] += mul_t(hot, acc_p[0:128], HIGHEST)

    returning = []
    for d in ORDER:
        for copy in inbound[d]:
            copy.wait()
        near_hot = hot_of(near[d, 512:520])
        near2 = split(near[d, 0:128])
        fill(there, mul(wp_t, stack3(near2)) + embed(emb[8:16], near_hot),
             near[d, 128:512], near[d, 512:520])
        live = (slot < counts[1 + d]).astype(F32)
        offsets = tuple(EDGE if k == d else 0.0 for k in range(3))
        ret[d] = block(fp[2 * d:2 * d + 1], fp[2 * d + 1:2 * d + 2], live, offsets)
        copy = pltpu.make_async_remote_copy(
            src_ref=ret.at[d, 0:520],
            dst_ref=back.at[d],
            send_sem=ret_send.at[d],
            recv_sem=ret_recv.at[d],
            device_id=neighbour(d, 1),
            device_id_type=MESH,
        )
        copy.start()
        returning.append(copy)
        proj_grad = ret[d, 0:128]
        gbuf[128:256] += outer3(near2, split(proj_grad))
        gbuf[272:280] += mul_t(near_hot, proj_grad, HIGHEST)

    center_grad = acc_c[0:128]
    gbuf[0:128] += outer3(sc2, split(center_grad))
    gbuf[264:272] += mul_t(hot, center_grad, HIGHEST)
    lane = lax.broadcasted_iota(jnp.int32, (1, atom_slots), 1)
    valid = (lane < atoms[0]).astype(F32)
    weighted = small[3:4] * valid
    wide_hot = (
        lax.broadcasted_iota(jnp.int32, (atom_slots, atom_slots), 0).astype(F32) == small[4:5]
    ).astype(F32)
    gbuf[792:800] += mul_t(
        rows_of([jnp.zeros_like(weighted), weighted], 8, atom_slots), wide_hot, HIGHEST
    )

    def finish():
        for copy in returning:
            copy.wait()
        vgrad_out[...] = acc_c[128:512] + acc_p[128:512] + (
            back[0, 128:512] + back[1, 128:512] + back[2, 128:512]
        )
        tail = acc_c[512:520] + acc_p[512:520] + (
            back[0, 512:520] + back[1, 512:520] + back[2, 512:520]
        )
        pos_out[...] = tail[0:3]
        self_energy = jnp.zeros((1, atom_slots), F32)
        for s in range(species_count):
            self_energy = self_energy + jnp.where(small[4:5] == float(s), ref_e[s], 0.0)
        energy_out[...] = tail[3:4] + valid * self_energy
        partner = acc_p[0:128] + (back[0, 0:128] + back[1, 0:128] + back[2, 0:128])
        sgrad_out[...] = mul(weight3(wc[...]), stack3(split(acc_c[0:128]))) + mul(
            weight3(wp[...]), stack3(split(partner))
        )

    start, length, sem = 0, rows, 0
    held = []
    for p, phase in enumerate(phases):
        size = phase[2]
        chunk = length // size
        copies = []
        for k in range(1, size):
            q, t, target = peer(phase, k)
            copy = pltpu.make_async_remote_copy(
                src_ref=gbuf.at[pl.ds(pl.multiple_of(start + t * chunk, 8), chunk)],
                dst_ref=landing[p].at[k - 1],
                send_sem=rs_send.at[sem],
                recv_sem=rs_recv.at[sem],
                device_id=target,
                device_id_type=MESH,
            )
            copy.start()
            copies.append(copy)
            sem += 1
        q = peer(phase, 0)[0]
        start = start + q * chunk
        mine = pl.ds(pl.multiple_of(start, 8), chunk)
        if p == min(1, n_phases - 1):
            finish()
        for copy in copies:
            copy.wait()
        total = gbuf[mine, :]
        for k in range(size - 1):
            total = total + landing[p][k]
        if p == n_phases - 1:
            agb[mine, :] = total * (1.0 / (sizes[0] * sizes[1] * sizes[2]))
        else:
            gbuf[mine, :] = total
        held.append((phase, start, chunk))
        length = chunk
    sem = 0
    for phase, start, chunk in reversed(held):
        mine = pl.ds(pl.multiple_of(start, 8), chunk)
        copies = []
        for k in range(1, phase[2]):
            copy = pltpu.make_async_remote_copy(
                src_ref=agb.at[mine],
                dst_ref=agb.at[mine],
                send_sem=ag_send.at[sem],
                recv_sem=ag_recv.at[sem],
                device_id=peer(phase, k)[2],
                device_id_type=MESH,
            )
            copy.start()
            copies.append(copy)
            sem += 1
        for copy in copies:
            copy.wait()
    wgrad_out[...] = agb[0:800]


def per_device(scalars, vectors, positions, species, atom_count, energy_weight, local_pairs,
               face_pairs, tile_counts, w_center, w_partner, w_radial, species_embed, w_mix,
               w_channel, w_read, w_out, species_energy, *, sizes):
    channels, atom_slots = scalars.shape[3:]
    small = jnp.concatenate(
        [
            positions[0, 0, 0],
            energy_weight[0, 0],
            species[0, 0].astype(F32),
            jnp.zeros((3, atom_slots), F32),
        ],
        axis=0,
    )
    width = face_pairs.shape[-1]
    total = sizes[0] * sizes[1] * sizes[2]
    rows = -(-800 // (8 * total)) * 8 * total
    phases = phase_list(sizes)
    landing, length, n_sems = [], rows, 0
    for _, _, size in phases:
        length //= size
        landing.append(pltpu.VMEM((size - 1, length, 128), F32))
        n_sems += size - 1
    vmem = pl.BlockSpec(memory_space=pltpu.VMEM)
    smem = pl.BlockSpec(memory_space=pltpu.SMEM)
    dma = pltpu.SemaphoreType.DMA
    energy, pos, sgrad, vgrad, wgrad = pl.pallas_call(
        functools.partial(kernel, sizes, rows, width),
        out_shape=(
            jax.ShapeDtypeStruct((1, atom_slots), F32),
            jax.ShapeDtypeStruct((3, atom_slots), F32),
            jax.ShapeDtypeStruct((channels, atom_slots), F32),
            jax.ShapeDtypeStruct((3 * channels, atom_slots), F32),
            jax.ShapeDtypeStruct((800, 128), F32),
        ),
        in_specs=[vmem] * 5 + [smem] * 2 + [vmem] * 8 + [smem],
        out_specs=(vmem,) * 5,
        scratch_shapes=[
            pltpu.VMEM((528, 256), B16),
            pltpu.VMEM((528, 256), B16),
            pltpu.VMEM((3, 520, 128), F32),
            pltpu.VMEM((3, 528, 128), F32),
            pltpu.VMEM((3, 520, 128), F32),
            pltpu.VMEM((528, 128), F32),
            pltpu.VMEM((528, 128), F32),
            pltpu.VMEM((rows, 128), F32),
            pltpu.VMEM((rows, 128), F32),
            pltpu.VMEM((128, 384), B16),
            pltpu.VMEM((128, 384), B16),
            pltpu.VMEM((256, 384), B16),
            pltpu.VMEM((128, 768), B16),
            pltpu.VMEM((128, 384), B16),
            pltpu.VMEM((128, 384), B16),
        ] + landing + [
            dma((9,)), dma((9,)), dma((3,)), dma((3,)),
            dma((n_sems,)), dma((n_sems,)), dma((n_sems,)), dma((n_sems,)),
        ],
        compiler_params=pltpu.CompilerParams(
            collective_id=0, has_side_effects=True, vmem_limit_bytes=40 * 1024 * 1024
        ),
    )(
        scalars[0, 0, 0],
        vectors[0, 0, 0].reshape(3 * channels, atom_slots),
        small,
        local_pairs[0, 0, 0],
        face_pairs[0, 0, 0].reshape(6, width),
        tile_counts[0, 0, 0],
        atom_count[0, 0],
        w_center,
        w_partner,
        w_radial,
        species_embed.reshape(-1, channels),
        w_mix,
        w_channel.reshape(-1, channels),
        w_read,
        w_out[None, :],
        species_energy,
    )
    weight_count = sum(
        w.size for w in (w_center, w_partner, w_radial, species_embed, w_mix, w_channel, w_read,
                         w_out, species_energy)
    )
    return (
        energy[None, None],
        pos[None, None, None],
        sgrad[None, None, None],
        vgrad.reshape(3, channels, atom_slots)[None, None, None],
        wgrad.reshape(-1)[:weight_count],
    )


def solution(mesh):
    sizes = tuple(mesh.shape[a] for a in AXES)
    here = ("gx", "gy", "gz")
    return jax.shard_map(
        functools.partial(per_device, sizes=sizes),
        mesh=mesh,
        in_specs=(
            P(*here, None, None),
            P(*here, None, None, None),
            P(*here, None, None),
            P(*here, None),
            P(*here),
            P(*here, None),
            P(*here, None, None),
            P(*here, None, None, None),
            P(*here, None),
        ) + (P(),) * 9,
        out_specs=(
            P(*here, None),
            P(*here, None, None),
            P(*here, None, None),
            P(*here, None, None, None),
            P(),
        ),
        check_vma=False,
    )
```

profile of v0, /device:TPU:0, one launch (start us, length us, event | category | flops | bytes accessed | tf_op | source)
XLA Modules:
  0.0 68.9 jit_solution(1217114418115615157)
XLA Ops:
  1.3 0.0 copy-start.16
  1.3 0.6 copy-done.16
  1.9 0.0 copy-start.14
  1.9 0.0 copy-start.13
  1.9 0.1 pad.3.clone
  2.0 0.6 copy-done.14
  2.6 0.0 copy-start.15
  2.6 0.7 copy-done.15
  3.3 0.0 copy-start.8
  3.3 0.1 maximum_maximum_fusion.refs_2_
  3.4 0.0 copy-done.13
  3.4 0.0 copy-start.7
  3.4 0.0 copy-start.9
  3.4 0.0 copy-start.10
  3.4 0.0 copy-start.11
  3.4 0.0 copy-start.12
  3.4 0.6 copy-done.8
  4.0 0.1 copy-done.7
  4.1 0.0 copy-done.9
  4.1 0.0 copy-done.10
  4.1 0.0 copy-done.11
  4.1 0.0 copy-done.12
  4.1 0.0 copy-start
  4.1 0.9 %copy-done = f32[1,1,1,3,128,128]{5,4,3,2,1,0:T(8,128)S(1)} copy-done((f32[1,1,1,3,128,128]{5,4,3,2,1,0:T(8,128)S(1)}, f32[1,1,1,3,128,128]{5,4,3,2,1,0:T(8,128)}, u32[]{:S(2)}) %copy-start) | copy-done | bytes 196632
  5.0 0.0 copy-start.1
  5.0 0.9 %copy-done.1 = f32[2,128,128]{2,1,0:T(8,128)S(1)} copy-done((f32[2,128,128]{2,1,0:T(8,128)S(1)}, f32[2,128,128]{2,1,0:T(8,128)}, u32[]{:S(2)}) %copy-start.1) | copy-done | bytes 131096
  5.9 0.0 copy-start.2
  5.9 0.8 %copy-done.2 = f32[1,1,1,128,128]{4,3,2,1,0:T(8,128)S(1)} copy-done((f32[1,1,1,128,128]{4,3,2,1,0:T(8,128)S(1)}, f32[1,1,1,128,128]{4,3,2,1,0:T(8,128)}, u32[]{:S(2)}) %copy-start.2) | copy-done | bytes 65560
  6.7 0.0 copy-start.3
  6.7 0.8 %copy-done.3 = f32[128,128]{1,0:T(8,128)S(1)} copy-done((f32[128,128]{1,0:T(8,128)S(1)}, f32[128,128]{1,0:T(8,128)}, u32[]{:S(2)}) %copy-start.3) | copy-done | bytes 65560
  7.6 0.0 copy-start.4
  7.6 0.8 %copy-done.4 = f32[128,128]{1,0:T(8,128)S(1)} copy-done((f32[128,128]{1,0:T(8,128)S(1)}, f32[128,128]{1,0:T(8,128)}, u32[]{:S(2)}) %copy-start.4) | copy-done | bytes 65560
  8.4 0.0 copy-start.5
  8.4 0.8 %copy-done.5 = f32[128,128]{1,0:T(8,128)S(1)} copy-done((f32[128,128]{1,0:T(8,128)S(1)}, f32[128,128]{1,0:T(8,128)}, u32[]{:S(2)}) %copy-start.5) | copy-done | bytes 65560
  9.3 0.0 copy-start.6
  9.3 0.8 %copy-done.6 = f32[128,128]{1,0:T(8,128)S(1)} copy-done((f32[128,128]{1,0:T(8,128)S(1)}, f32[128,128]{1,0:T(8,128)}, u32[]{:S(2)}) %copy-start.6) | copy-done | bytes 65560
  10.1 55.6 %shard_map.209 = (f32[1,128]{1,0:T(1,128)S(1)}, f32[3,128]{1,0:T(4,128)S(1)}, f32[128,128]{1,0:T(8,128)S(1)}, f32[384,128]{1,0:T(8,128)S(1)}, f32[800,128]{1,0:T(8,128)S(1)}) custom-call(f32[128,128]{1,0:T(8,128)S(1)} %bitcast.26, f32[384,128]{1,0:T(8,128)S(1)} %bitcast.23, f32[8,128]{1,0:T(8,128)S(1)} %maximum_maximum_fusion.refs_2_, ...), custom_call_target="tpu_custom_call" | custom-call | tf_op jit(solution)/shard_map/pallas_call | solution.py:416
  65.7 0.6 copy.23
  66.3 0.5 copy.32
  66.8 0.6 copy.33
  67.4 0.7 copy.34
  68.1 0.8 %copy.35 = f32[101512]{0:T(1024)} copy(f32[101512]{0:T(1024)S(1)} %bitcast.21) | data formatting | bytes 812096
  (4 shorter events, 0.0 us)
Async XLA Ops:
  1.3 0.7 copy-start.16
  1.9 0.7 copy-start.14
  1.9 1.4 %copy-start.13 = (s32[1,1,1,3,2,256]{5,4,3,2,1,0:T(2,128)S(1)}, s32[1,1,1,3,2,256]{5,4,3,2,1,0:T(2,128)}, u32[]{:S(2)}) copy-start(s32[1,1,1,3,2,256]{5,4,3,2,1,0:T(2,128)} %param.25) | copy-start | bytes 18436
  2.6 0.7 copy-start.15
  3.3 0.7 %copy-start.8 = (f32[2,8,128]{2,1,0:T(8,128)S(1)}, f32[2,8,128]{2,1,0:T(8,128)}, u32[]{:S(2)}) copy-start(f32[2,8,128]{2,1,0:T(8,128)} %param.30) | copy-start | bytes 24580
  3.4 0.7 %copy-start.7 = (s32[1,1,1,2,1024]{4,3,2,1,0:T(2,128)S(1)}, s32[1,1,1,2,1024]{4,3,2,1,0:T(2,128)}, u32[]{:S(2)}) copy-start(s32[1,1,1,2,1024]{4,3,2,1,0:T(2,128)} %param.24) | copy-start | bytes 24580
  3.4 0.7 %copy-start.9 = (f32[8,128]{1,0:T(8,128)S(1)}, f32[8,128]{1,0:T(8,128)}, u32[]{:S(2)}) copy-start(f32[8,128]{1,0:T(8,128)} %refs_9_.1) | copy-start | bytes 12292
  3.4 0.7 %copy-start.10 = (s32[1,1,1,4]{3,2,1,0:T(1,128)S(1)}, s32[1,1,1,4]{3,2,1,0:T(1,128)}, u32[]{:S(2)}) copy-start(s32[1,1,1,4]{3,2,1,0:T(1,128)} %param.26) | copy-start | bytes 52
  3.4 0.7 %copy-start.11 = (f32[128]{0:T(128)S(1)}, f32[128]{0:T(128)}, u32[]{:S(2)}) copy-start(f32[128]{0:T(128)} %param.34) | copy-start | bytes 1540
  3.4 0.7 %copy-start.12 = (f32[8]{0:T(128)S(1)}, f32[8]{0:T(128)}, u32[]{:S(2)}) copy-start(f32[8]{0:T(128)} %refs_15_.1) | copy-start | bytes 100
  4.1 0.9 %copy-start = (f32[1,1,1,3,128,128]{5,4,3,2,1,0:T(8,128)S(1)}, f32[1,1,1,3,128,128]{5,4,3,2,1,0:T(8,128)}, u32[]{:S(2)}) copy-start(f32[1,1,1,3,128,128]{5,4,3,2,1,0:T(8,128)} %param.19) | copy-start | bytes 589828
  5.0 0.9 %copy-start.1 = (f32[2,128,128]{2,1,0:T(8,128)S(1)}, f32[2,128,128]{2,1,0:T(8,128)}, u32[]{:S(2)}) copy-start(f32[2,128,128]{2,1,0:T(8,128)} %param.32) | copy-start | bytes 393220
  5.9 0.8 %copy-start.2 = (f32[1,1,1,128,128]{4,3,2,1,0:T(8,128)S(1)}, f32[1,1,1,128,128]{4,3,2,1,0:T(8,128)}, u32[]{:S(2)}) copy-start(f32[1,1,1,128,128]{4,3,2,1,0:T(8,128)} %param.18) | copy-start | bytes 196612
  6.7 0.8 %copy-start.3 = (f32[128,128]{1,0:T(8,128)S(1)}, f32[128,128]{1,0:T(8,128)}, u32[]{:S(2)}) copy-start(f32[128,128]{1,0:T(8,128)} %refs_7_.1) | copy-start | bytes 196612
  7.6 0.8 %copy-start.4 = (f32[128,128]{1,0:T(8,128)S(1)}, f32[128,128]{1,0:T(8,128)}, u32[]{:S(2)}) copy-start(f32[128,128]{1,0:T(8,128)} %refs_8_.1) | copy-start | bytes 196612
  8.4 0.8 %copy-start.5 = (f32[128,128]{1,0:T(8,128)S(1)}, f32[128,128]{1,0:T(8,128)}, u32[]{:S(2)}) copy-start(f32[128,128]{1,0:T(8,128)} %refs_11_.1) | copy-start | bytes 196612
  9.3 0.8 %copy-start.6 = (f32[128,128]{1,0:T(8,128)S(1)}, f32[128,128]{1,0:T(8,128)}, u32[]{:S(2)}) copy-start(f32[128,128]{1,0:T(8,128)} %refs_13_.1) | copy-start | bytes 196612
where the time goes:
time: 69.4 us; the launch traced here: 68.9 us
  Pallas kernels  55.6 us (80%)
  local copies, waits for them, and re-layouts  11.9 us (17%)
  between operations  1.34 us (2%)
    pallas_call x1, Pallas kernels, per_device(): pl.pallas_call(functools.partial(kernel, sizes, rows, width), out_shape=(...  55.6 us
    unnamed x40, local copies, waits for them, and re-layouts  11.8 us

commit v1 on v0

--- a/solution.py
+++ b/solution.py
@@ -73,12 +73,22 @@
 def kernel(sizes, rows, block_pairs, *refs):
     phases = phase_list(sizes)
     n_phases = len(phases)
-    (sc, vec, small, lp, fp, counts, atoms, wc, wp, wr, emb, wmix, wch, wread, wout, ref_e,
-     energy_out, pos_out, sgrad_out, vgrad_out, wgrad_out,
+    (sc_h, vec_h, pos_h, weight_h, kind_h, lp_h, fp_h, counts, atoms, wc_h, wp_h, wr, emb, wmix_h, wch_h, wread_h,
+     wout, ref_e, energy_out, pos_out, sgrad_out, vgrad_out, wgrad_out,
      here, there, near, ret, back, acc_c, acc_p, gbuf, agb,
-     mix_f, mix_b, ch_f, ch_b, read_f, read_b) = refs[:36]
-    landing = refs[36:36 + n_phases]
-    in_send, in_recv, ret_send, ret_recv, rs_send, rs_recv, ag_send, ag_recv = refs[36 + n_phases:]
+     mix_f, mix_b, ch_f, ch_b, read_f, read_b,
+     sc, vec, lp, fp, wc, wp, wmix, wch, wread, acc_out, acc_rad, small, pos_v, weight_v, kind_v) = refs[:53]
+    landing = refs[53:53 + n_phases]
+    (in_send, in_recv, ret_send, ret_recv, rs_send, rs_recv, ag_send, ag_recv,
+     load_sem) = refs[53 + n_phases:]
+    loads = []
+    for k, (src, dst) in enumerate(
+        ((pos_h, pos_v), (weight_h, weight_v), (kind_h, kind_v), (sc_h, sc), (wc_h, wc), (wp_h, wp), (vec_h, vec), (lp_h, lp), (wmix_h, wmix),
+         (wch_h, wch), (wread_h, wread), (fp_h, fp))
+    ):
+        copy = pltpu.make_async_copy(src, dst, load_sem.at[k])
+        copy.start()
+        loads.append(copy)
     atom_slots = sc.shape[1]
     channels = sc.shape[0]
     species_count = wr.shape[0]
@@ -107,10 +117,17 @@
         pl.semaphore_signal(barrier, inc=1, device_id=target, device_id_type=MESH)
     pl.semaphore_wait(barrier, len(greeted))
 
+    for copy in loads[:3]:
+        copy.wait()
+    coords = pos_v[...]
+    small[...] = rows_of(
+        [coords[0:1], coords[1:2], coords[2:3], weight_v[...], kind_v[...].astype(F32)],
+        8, atom_slots,
+    )
     inbound = {}
     for d in ORDER:
         copies = []
-        for part, (src, lo, hi) in enumerate(((small, 512, 520), (sc, 0, 128), (vec, 128, 512))):
+        for part, (src, lo, hi) in enumerate(((small, 512, 520), (sc_h, 0, 128), (vec_h, 128, 512))):
             copy = pltpu.make_async_remote_copy(
                 src_ref=src,
                 dst_ref=near.at[d, lo:hi],
@@ -123,6 +140,8 @@
             copies.append(copy)
         inbound[d] = copies
 
+    for copy in loads[3:]:
+        copy.wait()
     mix_b[...] = weight3(wmix[...])
     mix_f[...] = weight3(wmix[...].T)
     read_b[...] = weight3(wread[...])
@@ -130,13 +149,21 @@
     ch_b[...] = weight3(jnp.concatenate([wch[0:128], wch[128:256]], axis=1))
     ch_f[...] = weight3(jnp.concatenate([wch[0:128].T, wch[128:256].T], axis=0))
     radial = wr[...]
-    radial_t = jnp.concatenate([radial] * (channels // species_count), axis=0).T[:, 0:species_count]
+    rad_hi = radial.astype(B16).astype(F32)
+    rad_lo = (radial - rad_hi).astype(B16).astype(F32)
+    rad_zero = jnp.zeros_like(radial)
+    radial_t = jnp.concatenate(
+        [rad_hi, rad_hi, rad_lo] + [rad_zero] * (channels // species_count - 3), axis=0
+    ).T[:, 0:4 * species_count].astype(B16)
+    radial_b = weight3(jnp.concatenate([radial, rad_zero], axis=0))
     out_col = jnp.broadcast_to(wout[...], (channels, channels)).T[:, 0:1]
     wc_t = weight3(wc[...].T)
     wp_t = weight3(wp[...].T)
     gbuf[...] = jnp.zeros_like(gbuf)
     acc_c[...] = jnp.zeros_like(acc_c)
     acc_p[...] = jnp.zeros_like(acc_p)
+    acc_out[...] = jnp.zeros_like(acc_out)
+    acc_rad[...] = jnp.zeros_like(acc_rad)
 
     def hot_of(small_rows):
         row = lax.broadcasted_iota(jnp.int32, (species_count, atom_slots), 0).astype(F32)
@@ -185,8 +212,11 @@
         order = lax.broadcasted_iota(jnp.int32, (species_count, width), 0).astype(F32)
         t = (sq - order * spacing) / spacing
         basis = jnp.exp(-(t * t))
-        latent = at_i[0:128] + at_j[0:128] + jnp.dot(
-            radial_t, basis, precision=HIGHEST, preferred_element_type=F32
+        b_hi = basis.astype(B16).astype(F32)
+        b_lo = basis - b_hi
+        b_zero = jnp.zeros_like(basis)
+        latent = at_i[0:128] + at_j[0:128] + mul(
+            radial_t, jnp.concatenate([b_hi, b_lo, b_hi, b_zero], axis=0).astype(B16)
         )
         s1 = gate(latent)
         first = latent * s1
@@ -215,7 +245,7 @@
         halves = half_live * env * readout
         ge = half_live * pair_weight
         gr = ge * env
-        gbuf[792:800] += mul_t(rows_of([gr], 8, width), h, HIGHEST)
+        acc_out[...] += h * gr
         du = (out_col * gr) * (s3 * (1.0 + u * (1.0 - s3)))
         du2 = split(du)
         gbuf[664:792] += outer3(mixed2, du2)
@@ -235,8 +265,9 @@
         gbuf[280:408] += outer3(first2, dm2)
         dfirst = dsecond + mul(mix_b[...], stack3(dm2))
         dlat = dfirst * (s1 * (1.0 + latent * (1.0 - s1)))
-        gbuf[256:264] += mul_t(basis, dlat, HIGHEST)
-        dbasis = jnp.dot(radial, dlat, precision=HIGHEST, preferred_element_type=F32)
+        lat2 = split(dlat)
+        acc_rad[...] += outer3(lat2, split(jnp.concatenate([basis, b_zero], axis=0)))
+        dbasis = mul(radial_b, stack3(lat2))[0:species_count]
         dsq = jnp.sum(dbasis * basis * t, axis=0, keepdims=True) * (-2.0 / spacing)
         dsq = dsq + (dss - ge * readout * env * env) * (1.0 / (CUTOFF * CUTOFF))
         dcv = [n[k] * dac + dip * pv[k] for k in range(3)]
@@ -246,7 +277,6 @@
             + 2.0 * d[k] * dsq
             for k in range(3)
         ]
-        lat2 = split(dlat)
 
         def scatter(vector_parts, small_parts, one_hot):
             pieces = [lat2] + [split(v) for v in vector_parts]
@@ -285,7 +315,7 @@
              near[d, 128:512], near[d, 512:520])
         live = (slot < counts[1 + d]).astype(F32)
         offsets = tuple(EDGE if k == d else 0.0 for k in range(3))
-        ret[d] = block(fp[2 * d:2 * d + 1], fp[2 * d + 1:2 * d + 2], live, offsets)
+        ret[d] = block(fp[d, 0:1], fp[d, 1:2], live, offsets)
         copy = pltpu.make_async_remote_copy(
             src_ref=ret.at[d, 0:520],
             dst_ref=back.at[d],
@@ -309,9 +339,13 @@
     wide_hot = (
         lax.broadcasted_iota(jnp.int32, (atom_slots, atom_slots), 0).astype(F32) == small[4:5]
     ).astype(F32)
-    gbuf[792:800] += mul_t(
+    out_grad = jnp.broadcast_to(jnp.sum(acc_out[...], axis=1, keepdims=True), (128, 128)).T[0:8]
+    tail_row = lax.broadcasted_iota(jnp.int32, (8, 128), 0)
+    gbuf[792:800] = jnp.where(tail_row == 0, out_grad, 0.0) + mul_t(
         rows_of([jnp.zeros_like(weighted), weighted], 8, atom_slots), wide_hot, HIGHEST
     )
+    rad_wide = jnp.concatenate([acc_rad[...]] * 8, axis=1)
+    gbuf[256:264] = rad_wide.T[0:species_count]
 
     def finish():
         for copy in returning:
@@ -392,15 +426,6 @@
                face_pairs, tile_counts, w_center, w_partner, w_radial, species_embed, w_mix,
                w_channel, w_read, w_out, species_energy, *, sizes):
     channels, atom_slots = scalars.shape[3:]
-    small = jnp.concatenate(
-        [
-            positions[0, 0, 0],
-            energy_weight[0, 0],
-            species[0, 0].astype(F32),
-            jnp.zeros((3, atom_slots), F32),
-        ],
-        axis=0,
-    )
     width = face_pairs.shape[-1]
     total = sizes[0] * sizes[1] * sizes[2]
     rows = -(-800 // (8 * total)) * 8 * total
@@ -412,6 +437,7 @@
         n_sems += size - 1
     vmem = pl.BlockSpec(memory_space=pltpu.VMEM)
     smem = pl.BlockSpec(memory_space=pltpu.SMEM)
+    hbm = pl.BlockSpec(memory_space=pltpu.HBM)
     dma = pltpu.SemaphoreType.DMA
     energy, pos, sgrad, vgrad, wgrad = pl.pallas_call(
         functools.partial(kernel, sizes, rows, width),
@@ -422,7 +448,8 @@
             jax.ShapeDtypeStruct((3 * channels, atom_slots), F32),
             jax.ShapeDtypeStruct((800, 128), F32),
         ),
-        in_specs=[vmem] * 5 + [smem] * 2 + [vmem] * 8 + [smem],
+        in_specs=[hbm, hbm, hbm, hbm, hbm, hbm, hbm, smem, smem, hbm, hbm, vmem, vmem, hbm, hbm, hbm, vmem,
+                  smem],
         out_specs=(vmem,) * 5,
         scratch_shapes=[
             pltpu.VMEM((528, 256), B16),
@@ -440,19 +467,36 @@
             pltpu.VMEM((128, 768), B16),
             pltpu.VMEM((128, 384), B16),
             pltpu.VMEM((128, 384), B16),
+            pltpu.VMEM((128, 128), F32),
+            pltpu.VMEM((384, 128), F32),
+            pltpu.VMEM(local_pairs.shape[3:], jnp.int32),
+            pltpu.VMEM((3, 2, width), jnp.int32),
+            pltpu.VMEM((128, 128), F32),
+            pltpu.VMEM((128, 128), F32),
+            pltpu.VMEM((128, 128), F32),
+            pltpu.VMEM((256, 128), F32),
+            pltpu.VMEM((128, 128), F32),
+            pltpu.VMEM((128, width), F32),
+            pltpu.VMEM((128, 16), F32),
+            pltpu.VMEM((8, atom_slots), F32),
+            pltpu.VMEM((3, atom_slots), F32),
+            pltpu.VMEM((1, atom_slots), F32),
+            pltpu.VMEM((1, atom_slots), jnp.int32),
         ] + landing + [
             dma((9,)), dma((9,)), dma((3,)), dma((3,)),
-            dma((n_sems,)), dma((n_sems,)), dma((n_sems,)), dma((n_sems,)),
+            dma((n_sems,)), dma((n_sems,)), dma((n_sems,)), dma((n_sems,)), dma((12,)),
         ],
         compiler_params=pltpu.CompilerParams(
-            collective_id=0, has_side_effects=True, vmem_limit_bytes=40 * 1024 * 1024
+            collective_id=0, has_side_effects=True, vmem_limit_bytes=63 * 1024 * 1024
         ),
     )(
         scalars[0, 0, 0],
         vectors[0, 0, 0].reshape(3 * channels, atom_slots),
-        small,
+        positions[0, 0, 0],
+        energy_weight[0, 0],
+        species[0, 0],
         local_pairs[0, 0, 0],
-        face_pairs[0, 0, 0].reshape(6, width),
+        face_pairs[0, 0, 0],
         tile_counts[0, 0, 0],
         atom_count[0, 0],
         w_center,

time: 69.4 us -> 64.1 us (0.924)
  local copies, waits for them, and re-layouts: 11.9 us -> 7.52 us
    unnamed x40 -> x10, local copies, waits for them, and re-layouts: 11.8 us -> 7.52 us
where the time goes in v1:
time: 64.1 us; the launch traced here: 63.9 us
  Pallas kernels  55 us (86%)
  local copies, waits for them, and re-layouts  7.52 us (12%)
  between operations  1.31 us (2%)
    pallas_call x1, Pallas kernels, per_device(): pl.pallas_call(functools.partial(kernel, sizes, rows, width), out_shape=(...  55 us
    unnamed x10, local copies, waits for them, and re-layouts  7.52 us

profile of v1, /device:TPU:0, one launch (start us, length us, event | category | flops | bytes accessed | tf_op | source)
XLA Modules:
  0.0 63.9 jit_solution(14526836264279160659)
XLA Ops:
  1.3 0.0 copy-start.1
  1.3 0.7 %copy-done.1 = f32[1,1,1,3,128]{4,2,3,1,0:T(1,128)S(1)} copy-done((f32[1,1,1,3,128]{4,2,3,1,0:T(1,128)S(1)}, f32[1,1,1,3,128]{4,2,3,1,0:T(1,128)}, u32[]{:S(2)}) %copy-start.1) | copy-done | bytes 1560
  2.0 0.6 copy.26
  2.5 55.0 %shard_map.209 = (f32[1,128]{1,0:T(1,128)}, f32[3,128]{1,0:T(4,128)}, f32[128,128]{1,0:T(8,128)}, f32[384,128]{1,0:T(8,128)}, f32[800,128]{1,0:T(8,128)}) custom-call(f32[128,128]{1,0:T(8,128)} %bitcast.26, f32[384,128]{1,0:T(8,128)} %bitcast.23, f32[3,128]{1,0:T(4,128)} %bitcast.29, f32[1,128]{1,0:T(1,128)} %bitcast.32, s32[1,128]{1,0:T(1,128)} %bitcast.33, ...), custom_call_target="tpu_custom_call" | custom-call | tf_op jit(solution)/shard_map/pallas_call | solution.py:442
  57.6 0.0 copy-start
  57.6 1.3 %copy.23 = f32[1,1,1,3,128]{4,2,3,1,0:T(1,128)} copy(f32[1,1,1,3,128]{4,3,2,1,0:T(4,128)} %bitcast.31) | data formatting | bytes 3072
  58.9 1.1 %copy.32 = f32[1,1,1,128]{3,2,1,0:T(1,128)} copy(f32[1,1,1,128]{3,2,1,0:T(1,128)} %bitcast.36) | data formatting | bytes 1024
  60.0 1.5 %copy.33 = f32[1,1,1,128,128]{4,3,2,1,0:T(8,128)} copy(f32[1,1,1,128,128]{4,3,2,1,0:T(8,128)} %bitcast.25) | data formatting | bytes 131072
  61.5 1.6 %copy.34 = f32[1,1,1,3,128,128]{5,4,3,2,1,0:T(8,128)} copy(f32[1,1,1,3,128,128]{5,4,3,2,1,0:T(8,128)} %bitcast.22) | data formatting | bytes 393216
  63.1 0.0 copy-done
  63.1 0.8 %copy.35 = f32[101512]{0:T(1024)} copy(f32[101512]{0:T(1024)S(1)} %bitcast.21) | data formatting | bytes 812096
Async XLA Ops:
  1.3 0.7 %copy-start.1 = (f32[1,1,1,3,128]{4,2,3,1,0:T(1,128)S(1)}, f32[1,1,1,3,128]{4,2,3,1,0:T(1,128)}, u32[]{:S(2)}) copy-start(f32[1,1,1,3,128]{4,2,3,1,0:T(1,128)} %param.20) | copy-start | bytes 4612
  57.6 5.5 %copy-start = (f32[800,128]{1,0:T(8,128)S(1)}, f32[800,128]{1,0:T(8,128)}, u32[]{:S(2)}) copy-start(f32[800,128]{1,0:T(8,128)} %get-tuple-element.14) | copy-start | bytes 1228804
